TPU v7x, 512 devices: a whole 4x4x16 slice. The times are simulated.
512 devices in a mesh: group: 32 (over z_lo, x), module: 16 (over z_hi, y, core).
Axes of the slice: x: 4, y: 4, z: 16 (z_hi: 2, z_lo: 8; z = z_hi * 8 + z_lo), core: 2. Of those that a mesh axis runs over, the one named last changes fastest.
Arguments:
- train_grads: bfloat16 [32768, 16, 1024], P(('group', 'module')), may hold values from -6 to 6
- query_grads: bfloat16 [32, 32, 16, 1024], P('group', None, 'module'), may hold values from -6 to 6
- basis_out: bfloat16 [16, 32, 32], P('module'), may hold values from -1 to 1
- basis_in: bfloat16 [16, 32, 32], P('module'), may hold values from -1 to 1
- eigenvalues: float32 [16, 1024], P('module'), may hold values from 0.05 to 5
- owner_groups: int32 [4], replicated, may hold values from 0 to 31, as said below
- module_order: int32 [16], replicated, may hold values from 0 to 15, each once
Outputs:
- scores: float32 [32768, 128], P(('group', 'module'))
Inputs may be any that keep to these rules, and one draw needn't show every extreme that they name: `owner_groups`: 4 different groups, the first and the last group among them. `module_order`: each module exactly once.
All inputs are finite; a program needn't handle non-finite values.
Results may differ from a plain program's by a relative error of at most 0.0037.
Values may be sent and summed in bfloat16 or wider, within the bound.
A program may use at most 64 MiB of HBM per device.

v0:
```python
import math

import jax
import jax.numpy as jnp
from jax import lax
from jax.sharding import PartitionSpec as P


def build_rotator(basis_out, basis_in):
    breadth = basis_out.shape[-1]
    product = (
        basis_out.astype(jnp.float32)[..., :, None, :, None]
        * basis_in.astype(jnp.float32)[..., None, :, None, :]
    )
    return product.reshape(basis_out.shape[:-2] + (breadth * breadth, breadth * breadth)).astype(
        jnp.bfloat16
    )


def local(train_grads, query_grads, basis_out, basis_in, eigenvalues, owner_groups, module_order):
    ex_rows, modules, width = train_grads.shape
    module_devices = lax.axis_size("module")
    slots_dev = modules // module_devices
    rotator = build_rotator(basis_out, basis_in)
    damping = 0.1 * jnp.mean(eigenvalues, axis=1, keepdims=True)
    divisor = eigenvalues + damping
    ordered = jnp.take(train_grads, module_order, axis=1)
    everyone = lax.all_gather(query_grads, "group", axis=0, tiled=True)
    picked = jnp.take(everyone, owner_groups, axis=0)
    queries = picked.reshape(-1, slots_dev, width)
    asked = (
        jnp.einsum("qtw,twv->qtv", queries, rotator, preferred_element_type=jnp.float32)
        / divisor[None]
    ).astype(jnp.bfloat16)
    factor = 1.0 / math.sqrt(modules * width)
    moved = lax.all_to_all(
        ordered.reshape(ex_rows, module_devices, slots_dev, width),
        "module",
        split_axis=1,
        concat_axis=0,
        tiled=True,
    )
    moved = moved.reshape(ex_rows * module_devices, slots_dev, width)
    turned = jnp.einsum("gtw,twv->gtv", moved, rotator, preferred_element_type=jnp.float32).astype(
        jnp.bfloat16
    )
    summed = lax.psum_scatter(
        jnp.einsum("gtv,qtv->gq", turned, asked, preferred_element_type=jnp.float32),
        "module",
        scatter_dimension=0,
        tiled=True,
    )
    return summed * factor


def solution(mesh):
    in_specs = (
        P(("group", "module"), None, None),
        P("group", None, "module", None),
        P("module", None, None),
        P("module", None, None),
        P("module", None),
        P(),
        P(),
    )
    out_specs = P(("group", "module"), None)
    return jax.shard_map(local, mesh=mesh, in_specs=in_specs, out_specs=out_specs, check_vma=False)
```

profile of v0, /device:TPU:1, one launch (start us, length us, event | category | flops | bytes accessed | tf_op | source)
XLA Modules:
  0.0 432.3 jit_solution(14331242185848349895)
XLA Ops:
  6.5 0.0 copy-start
  6.5 0.8 compare_select_fusion.1
  7.3 0.7 compare_and_fusion.1
  8.0 0.1 copy-done
  8.1 7.9 %gather_fusion = bf16[16,64,1024]{2,0,1:T(8,128)(2,1)} fusion(bf16[64,16,1024]{2,1,0:T(8,128)(2,1)S(1)} %copy-done, s32[1024]{0:T(1024)S(1)} %pad_clamp_fusion.1), kind=kCustom, calls=%fused_computation | custom fusion | bytes 4194368 | tf_op jit(solution)/shard_map/jit(_take)/gather | solution.py:27
  16.0 1.8 bitcast_select_fusion
  17.9 2.5 copy.9
  20.3 19.4 %all-to-all-start = ((bf16[64,16,1,1024]{3,0,2,1:T(8,128)(2,1)}), bf16[64,16,1,1024]{3,0,2,1:T(8,128)(2,1)}, u32[]{:S(2)}, u32[]{:S(2)}) async-start(bf16[64,16,1,1024]{3,0,2,1:T(8,128)(2,1)} %copy.9), calls=%async_computation | async-start | bytes 4194304 | tf_op jit(solution)/shard_map/all_to_all | solution.py:36
  39.7 0.0 all-gather.2.cloned.1.call-start
  39.7 0.7 all-gather.2.cloned.1.call-update
  40.4 0.2 reduce-scatter.2.cloned.1.call-start
  40.7 0.0 copy-done.2
  40.7 5.3 %multiply_convert_fusion = bf16[32,32,32,32]{3,2,1,0:T(8,128)(2,1)} fusion(f32[32,32]{1,0:T(8,128)S(1)} %get-tuple-element.5, f32[32,32]{1,0:T(8,128)S(1)} %get-tuple-element.6), kind=kLoop, calls=%fused_computation.2 | loop fusion | flops 2097152 | bytes 2105344 | tf_op jit(solution)/shard_map/convert_element_type | solution.py:15
  46.0 12.4 %convert_element_type.38 = bf16[1024,1024]{1,0:T(8,128)(2,1)} reshape(bf16[32,32,32,32]{3,2,1,0:T(8,128)(2,1)} %multiply_convert_fusion) | data formatting | bytes 4194304 | tf_op jit(solution)/shard_map/convert_element_type | solution.py:15
  58.4 0.6 reduce_sum.9
  59.7 223.2 %all-gather.2.cloned.1.call-done = bf16[32,32,1,1024]{3,1,2,0:T(8,128)(2,1)} async-done(((bf16[1,32,1,1024]{3,1,2,0:T(8,128)(2,1)}), bf16[32,32,1,1024]{3,1,2,0:T(8,128)(2,1)}) %all-gather.2.cloned.1.call-update) | async-done | bytes 2097168 | tf_op jit(solution)/shard_map/all_gather | solution.py:28
  282.9 2.2 gather_fusion.1
  285.1 0.1 bitcast_select_fusion.1
  285.2 2.4 fusion.7
  287.6 0.0 all-to-all-done
  287.6 6.8 %fusion = f32[1024,128]{1,0:T(8,128)} fusion(bf16[128,1024]{0,1:T(8,128)(2,1)S(1)} %fusion.7, bf16[1024,1024]{1,0:T(8,128)(2,1)} %convert_element_type.38, bf16[1024,1024]{1,0:T(8,128)(2,1)} %bitcast.6), kind=kOutput, calls=%fused_computation.3 | convolution fusion | flops 2416967680 | bytes 4980736 | tf_op jit(solution)/shard_map/gtv,qtv->gq/dot_general | solution.py:48
  294.4 0.0 reduce-scatter.2.cloned.1.call-update
  294.4 129.7 %reduce-scatter.2.cloned.1.call-done = f32[64,128]{1,0:T(8,128)} async-done(((f32[1024,128]{1,0:T(8,128)}), f32[64,128]{1,0:T(8,128)}) %reduce-scatter.2.cloned.1.call-update) | async-done | bytes 32784 | tf_op jit(solution)/shard_map/reduce_scatter | solution.py:47
  424.1 1.4 broadcast_multiply_fusion
  (13 shorter events, 0.1 us)
Async XLA Ops:
  6.5 1.6 copy-start
  20.3 20.3 %copy-start.2 = (bf16[1,32,32]{2,1,0:T(8,128)(2,1)S(1)}, bf16[1,32,32]{2,1,0:T(8,128)(2,1)}, u32[]{:S(2)}) copy-start(bf16[1,32,32]{2,1,0:T(8,128)(2,1)} %param.10) | copy-start | bytes 6148
  20.3 20.3 %copy-start.3 = (bf16[1,32,32]{2,1,0:T(8,128)(2,1)S(1)}, bf16[1,32,32]{2,1,0:T(8,128)(2,1)}, u32[]{:S(2)}) copy-start(bf16[1,32,32]{2,1,0:T(8,128)(2,1)} %param.9) | copy-start | bytes 6148
  20.3 267.2 %all-to-all-start = ((bf16[64,16,1,1024]{3,0,2,1:T(8,128)(2,1)}), bf16[64,16,1,1024]{3,0,2,1:T(8,128)(2,1)}, u32[]{:S(2)}, u32[]{:S(2)}) async-start(bf16[64,16,1,1024]{3,0,2,1:T(8,128)(2,1)} %copy.9), calls=%async_computation | async-start | bytes 4194304 | tf_op jit(solution)/shard_map/all_to_all | solution.py:36
  39.7 243.2 %all-gather.2.cloned.1.call-start = ((), (), s32[]{:S(2)}) async-start(), calls=%async_computation.2 | async-start | bytes 2162688 | tf_op jit(solution)/shard_map/all_gather | solution.py:28
  40.4 383.7 %reduce-scatter.2.cloned.1.call-start = ((), (), s32[]{:S(2)}) async-start(), calls=%async_computation.3 | async-start | bytes 557056 | tf_op jit(solution)/shard_map/reduce_scatter | solution.py:47
  46.0 12.4 %copy-start.1 = (f32[1,1024]{1,0:T(1,128)S(1)}, f32[1,1024]{1,0:T(1,128)}, u32[]{:S(2)}) copy-start(f32[1,1024]{1,0:T(1,128)} %param.11) | copy-start | bytes 12292
  46.0 13.7 %copy-start.4 = (s32[4]{0:T(128)S(1)}, s32[4]{0:T(128)}, u32[]{:S(2)}) copy-start(s32[4]{0:T(128)} %param.12) | copy-start | bytes 52
Sparse Core Ops, SparseCore 0:
  42.6 240.2 all-gather.1
  294.5 129.5 reduce-scatter.1
where the time goes:
time: 433 us; the launch traced here: 432 us
  waiting for transfers between devices  354 us (82%)
  local copies, waits for them, and re-layouts  25.1 us (6%)
  starting transfers between devices  19.6 us (5%)
  between operations  14.2 us (3%)
  other arithmetic  10.7 us (2%)
  matrix products  9.18 us (2%)
    all_gather x1, waiting for transfers between devices, local(): everyone = lax.all_gather(query_grads, 'group', axis=0, tiled=True)  223 us
    reduce_scatter x1, waiting for transfers between devices, local(): lax.psum_scatter(jnp.einsum('gtv,qtv->gq', turned, asked, preferred_eleme...  130 us
    all_to_all x1, starting transfers between devices, local(): lax.all_to_all(ordered.reshape(ex_rows, module_devices, slots_dev, width)...  19.4 us
    convert_element_type x1, local copies, waits for them, and re-layouts, build_rotator(): product.reshape(basis_out.shape[:-2] + (breadth * breadth, breadth * brea...  12.4 us
  transfers between devices with their start and end apart: 3, of which 2 were waited for; matrix products, arithmetic and copies ran while one was open for 5% of the time, Pallas kernels for 0%

commit v1 on v0

v1 whole, which is shorter than its diff:
```python
import math

import jax
import jax.numpy as jnp
from jax import lax
from jax.sharding import PartitionSpec as P


def build_rotator(basis_out, basis_in):
    breadth = basis_out.shape[-1]
    product = (
        basis_out.astype(jnp.float32)[:, None, :, None]
        * basis_in.astype(jnp.float32)[None, :, None, :]
    )
    return product.reshape(breadth * breadth, breadth * breadth).astype(jnp.bfloat16)


def local(train_grads, query_grads, basis_out, basis_in, eigenvalues, owner_groups, module_order):
    ex_rows, modules, width = train_grads.shape
    owners, held = owner_groups.shape[0], query_grads.shape[1]
    groups = lax.axis_size("group")
    rotator = build_rotator(basis_out[0], basis_in[0])
    divisor = eigenvalues + 0.1 * jnp.mean(eigenvalues, axis=1, keepdims=True)
    owned = owner_groups == lax.axis_index("group")
    offered = jnp.where(owned[:, None, None], query_grads[0, :, 0][None], 0)
    mine = lax.psum_scatter(
        offered.reshape(owners * held, width), "group", scatter_dimension=0, tiled=True
    )
    asked = (jnp.dot(mine, rotator, preferred_element_type=jnp.float32) / divisor).astype(
        jnp.bfloat16
    )
    back = lax.dot_general(
        asked, rotator, (((1,), (1,)), ((), ())), preferred_element_type=jnp.float32
    ).astype(jnp.bfloat16)
    everywhere = lax.all_gather(back, ("group", "module"), axis=0, tiled=True)
    everywhere = everywhere.reshape(groups, modules, owners * held // groups, width)
    ordered = jnp.take(train_grads, module_order, axis=1)
    scores = jnp.einsum("esw,gsqw->egq", ordered, everywhere, preferred_element_type=jnp.float32)
    return scores.reshape(ex_rows, owners * held) * (1.0 / math.sqrt(modules * width))


def solution(mesh):
    in_specs = (
        P(("group", "module"), None, None),
        P("group", None, "module", None),
        P("module", None, None),
        P("module", None, None),
        P("module", None),
        P(),
        P(),
    )
    out_specs = P(("group", "module"), None)
    return jax.shard_map(local, mesh=mesh, in_specs=in_specs, out_specs=out_specs, check_vma=False)
```

time: 433 us -> 1310 us (3.03)
  waiting for transfers between devices: 354 us -> 1230 us
  starting transfers between devices: 19.6 us -> 0.04 us
    all_gather x1, waiting for transfers between devices: 223 us -> 814 us  [local(): everywhere = lax.all_gather(back, ('group', 'module'), axis=0, tiled=True)]
    unnamed x2 -> x3, waiting for transfers between devices: 0.7 us -> 415 us
    reduce_scatter x1 -> x0, waiting for transfers between devices: 130 us -> none  [local(): lax.psum_scatter(jnp.einsum('gtv,qtv->gq', turned, asked, preferred_eleme...]
    all_to_all x1 -> x0, starting transfers between devices: 19.4 us -> none  [local(): lax.all_to_all(ordered.reshape(ex_rows, module_devices, slots_dev, width)...]
  transfers between devices with their start and end apart: 3 -> 2, of which waited for: 2 -> 2; matrix products, arithmetic and copies ran while one was open for 5% -> 2% of each run, Pallas kernels for 0% -> 0%
where the time goes in v1:
time: 1310 us; the launch traced here: 1300 us
  waiting for transfers between devices  1230 us (94%)
  local copies, waits for them, and re-layouts  34.7 us (3%)
  between operations  14.8 us (1%)
    all_gather x1, waiting for transfers between devices, local(): everywhere = lax.all_gather(back, ('group', 'module'), axis=0, tiled=True)  814 us
    unnamed x3, waiting for transfers between devices  415 us
  transfers between devices with their start and end apart: 2, of which 2 were waited for; matrix products, arithmetic and copies ran while one was open for 2% of the time, Pallas kernels for 0%

profile of v1, /device:TPU:1, one launch (start us, length us, event | category | flops | bytes accessed | tf_op | source)
XLA Modules:
  0.0 1300.7 jit_solution(6297640586072213464)
XLA Ops:
  6.5 0.0 copy-start
  6.5 0.0 all-reduce.3.cloned.1.call-start
  6.5 0.8 broadcast_compare_fusion
  7.3 0.1 broadcast_in_dim.47
  7.4 0.1 broadcast_in_dim.48
  7.5 1.6 bitcast_select_fusion
  9.1 0.0 all-reduce.3.cloned.1.call-update
  9.2 0.0 all-gather.3.cloned.1.call-start
  9.2 0.7 bitcast_convert_fusion
  9.9 5.3 multiply_convert_fusion
  15.2 12.4 convert_element_type.39
  27.6 1.3 dynamic-slice
  29.5 0.0 copy-done.1
  29.5 0.6 reduce_sum.9
  30.8 415.2 %all-reduce.3.cloned.1.call-done = bf16[128,1024]{1,0:T(8,128)(2,1)} async-done(((bf16[128,1024]{1,0:T(8,128)(2,1)}), bf16[128,1024]{1,0:T(8,128)(2,1)}) %all-reduce.3.cloned.1.call-update) | async-done | bytes 262160
  446.0 3.8 fusion.9
  449.7 0.0 all-gather.3.cloned.1.call-update
  449.8 0.0 copy-done
  449.8 7.9 gather_fusion
  457.7 3.2 select_bitcast_fusion
  460.9 813.7 %all-gather.3.cloned.1.call-done = bf16[512,4,1024]{2,1,0:T(4,128)(2,1)} async-done(((bf16[1,4,1024]{2,1,0:T(4,128)(2,1)}), bf16[512,4,1024]{2,1,0:T(4,128)(2,1)}) %all-gather.3.cloned.1.call-update) | async-done | bytes 4194320 | tf_op jit(solution)/shard_map/all_gather | solution.py:35
  1274.6 6.1 copy.21
  1280.7 6.9 dot_general.16
  1287.6 6.3 fusion.5
  (7 shorter events, 0.0 us)
Async XLA Ops:
  6.5 443.3 %copy-start = (bf16[64,16,1024]{2,1,0:T(8,128)(2,1)S(1)}, bf16[64,16,1024]{2,1,0:T(8,128)(2,1)}, u32[]{:S(2)}) copy-start(bf16[64,16,1024]{2,1,0:T(8,128)(2,1)} %param.7) | copy-start | bytes 6291460
  6.5 439.4 %all-reduce.3.cloned.1.call-start = ((), (), s32[]{:S(2)}) async-start(), calls=%async_computation.1 | async-start | bytes 524288
  9.2 1265.5 %all-gather.3.cloned.1.call-start = ((), (), s32[]{:S(2)}) async-start(), calls=%async_computation | async-start | bytes 4202496 | tf_op jit(solution)/shard_map/all_gather | solution.py:35
  15.2 14.3 %copy-start.1 = (f32[1,1024]{1,0:T(1,128)S(1)}, f32[1,1024]{1,0:T(1,128)}, u32[]{:S(2)}) copy-start(f32[1,1024]{1,0:T(1,128)} %param.11) | copy-start | bytes 12292
  446.0 3.8 copy-start.2
Sparse Core Ops, SparseCore 0:
  10.3 435.6 all-reduce.2
  449.9 824.7 all-gather.2

commit v2 on v1

v2 whole, which is shorter than its diff:
```python
import functools
import math

import jax
import jax.numpy as jnp
from jax import lax
from jax.experimental import pallas as pl
from jax.experimental.pallas import tpu as pltpu
from jax.sharding import PartitionSpec as P

ZH, Y, C = 2, 4, 2
X = 4
F32, BF16 = jnp.float32, jnp.bfloat16


def kernel(
    dims,
    train_ref,
    query_ref,
    bout_ref,
    bin_ref,
    eig_ref,
    owner_ref,
    order_ref,
    out_ref,
    perm,
    ordered,
    gathered,
    rot,
    turned,
    bases,
    eigs,
    raw,
    offer,
    offered,
    chosen,
    asked,
    part,
    parts,
    s1s,
    s1r,
    s2s,
    s2r,
    s3s,
    s3r,
    s4s,
    s4r,
    sgs,
    sgr,
    sbs,
    sbr,
    sps,
    spr,
):
    zl_n, x_n, zh_n, y_n, c_n = dims
    t_n = y_n * c_n
    z_n = zh_n * zl_n
    rows, modules, width = train_ref.shape
    held = query_ref.shape[0]
    piece = width // zl_n
    group, module = lax.axis_index("group"), lax.axis_index("module")
    zl, xi = lax.div(group, x_n), lax.rem(group, x_n)
    zh, ti = lax.div(module, t_n), lax.rem(module, t_n)
    yi = lax.div(ti, c_n)
    zi = zh * zl_n + zl

    def at(z=None, x=None, t=None):
        z = zi if z is None else z
        x = xi if x is None else x
        t = ti if t is None else t
        return (lax.rem(z, zl_n) * x_n + x, lax.div(z, zl_n) * t_n + t)

    def remote(src, dst, send, recv, where):
        return pltpu.make_async_remote_copy(
            src_ref=src,
            dst_ref=dst,
            send_sem=send,
            recv_sem=recv,
            device_id=where,
            device_id_type=pl.DeviceIdType.MESH,
        )

    barrier = pltpu.get_barrier_semaphore()

    def greet(where):
        pl.semaphore_signal(
            barrier, inc=1, device_id=where, device_id_type=pl.DeviceIdType.MESH
        )

    @pl.loop(1, z_n)
    def _(i):
        greet(at(z=lax.rem(zi + i, z_n)))

    @pl.loop(1, x_n)
    def _(i):
        greet(at(x=lax.rem(xi + i, x_n)))

    @pl.loop(1, t_n)
    def _(i):
        greet(at(t=lax.rem(ti + i, t_n)))

    batch = 16
    span = batch * modules
    for s in range(modules):
        lane = lax.broadcasted_iota(jnp.int32, (batch, span), 1)
        row = lax.broadcasted_iota(jnp.int32, (batch, span), 0)
        hit = lane == row * modules + order_ref[s]
        perm[pl.ds(s * batch, batch), :] = jnp.where(hit, 1.0, 0.0).astype(BF16)
    for b in range(rows // batch):
        block = train_ref[pl.ds(b * batch, batch)].reshape(span, width)
        moved = jnp.dot(perm[...], block, preferred_element_type=F32).astype(BF16)
        ordered[:, pl.ds(b * batch, batch), :] = moved.reshape(modules, batch, width)

    bases[zh] = jnp.zeros(bases.shape[1:], BF16)
    bases[zh, 0, :, : bout_ref.shape[1]] = bout_ref[...]
    bases[zh, 1, :, : bin_ref.shape[1]] = bin_ref[...]
    eigs[zh] = eig_ref[...]

    pl.semaphore_wait(barrier, z_n + x_n + t_n - 3)

    def send1(z):
        return remote(
            query_ref.at[:, pl.ds(pl.multiple_of(z * piece, piece), piece)],
            raw.at[zl],
            s1s.at[z],
            s1r.at[zl],
            at(z=zh * zl_n + z),
        )

    @pl.loop(1, zl_n)
    def _(i):
        send1(lax.rem(zl + i, zl_n)).start()

    other = zh_n - 1 - zh
    twins = [
        remote(bases.at[zh], bases.at[zh], sbs.at[0], sbr.at[0], at(z=other * zl_n + zl)),
        remote(eigs.at[zh], eigs.at[zh], sbs.at[1], sbr.at[1], at(z=other * zl_n + zl)),
    ]
    for twin in twins:
        twin.start()

    def send_g(t, h):
        return remote(
            ordered.at[h * t_n + t],
            gathered.at[h, pl.ds(pl.multiple_of(ti * rows, rows), rows)],
            sgs.at[t, h],
            sgr.at[ti, h],
            at(t=t),
        )

    def got_g(t, h):
        return remote(
            ordered.at[h * t_n + t],
            gathered.at[h, pl.ds(pl.multiple_of(t * rows, rows), rows)],
            sgs.at[t, h],
            sgr.at[t, h],
            at(t=t),
        )

    @pl.loop(1, t_n)
    def _(i):
        for h in range(zh_n):
            send_g(jnp.bitwise_xor(ti, i), h).start()

    for h in range(zh_n):
        gathered[h, pl.ds(pl.multiple_of(ti * rows, rows), rows)] = ordered[h * t_n + ti]

    def build(h):
        side = bout_ref.shape[1]
        lane = lax.broadcasted_iota(jnp.int32, (bases.shape[3], width), 1)
        row = lax.broadcasted_iota(jnp.int32, (bases.shape[3], width), 0)
        wide = jnp.where(lax.div(lane, side) == row, 1.0, 0.0).astype(BF16)
        tiled = jnp.where(lax.rem(lane, side) == row, 1.0, 0.0).astype(BF16)
        outer = jnp.dot(bases[h, 0], wide, preferred_element_type=F32)
        inner = jnp.dot(bases[h, 1], tiled, preferred_element_type=F32)
        for a in range(side):
            rot[h, pl.ds(a * side, side), :] = (outer[a : a + 1] * inner).astype(BF16)

    build(zh)

    raw[zl] = query_ref[:, pl.ds(pl.multiple_of(zl * piece, piece), piece)]

    @pl.loop(1, zl_n)
    def _(i):
        z = lax.rem(zl + i, zl_n)
        remote(raw.at[z], raw.at[z], s1s.at[z], s1r.at[z], at()).wait_recv()

    for k in range(x_n):
        offer[k] = raw[lax.div(owner_ref[k], x_n)]

    def send2(x):
        return remote(offer.at[x], offered.at[xi], s2s.at[x], s2r.at[xi], at(x=x))

    @pl.loop(1, x_n)
    def _(i):
        send2(lax.rem(xi + i, x_n)).start()

    offered[xi] = offer[xi]

    @pl.loop(1, x_n)
    def _(i):
        x = lax.rem(xi + i, x_n)
        remote(offer.at[x], offered.at[x], s2s.at[x], s2r.at[x], at()).wait_recv()

    lines = pl.ds(pl.multiple_of(xi * held, held), held)
    chosen[zh, lines, pl.ds(pl.multiple_of(zl * piece, piece), piece)] = offered[
        lax.rem(owner_ref[xi], x_n)
    ]

    def chunk(z, k):
        return chosen.at[
            lax.div(z, zl_n),
            pl.ds(pl.multiple_of(k * held, held), held),
            pl.ds(pl.multiple_of(lax.rem(z, zl_n) * piece, piece), piece),
        ]

    def send3(z):
        return remote(chunk(zi, xi), chunk(zi, xi), s3s.at[z], s3r.at[zi], at(z=z))

    @pl.loop(1, z_n)
    def _(i):
        send3(lax.rem(zi + i, z_n)).start()

    for twin in twins:
        twin.wait_send()
    for i, buf in enumerate((bases, eigs)):
        remote(buf.at[other], buf.at[other], sbs.at[i], sbr.at[i], at()).wait_recv()
    build(other)

    wide_n = 256
    tiles = width // wide_n

    def turn(y):
        @pl.loop(0, zh_n * tiles)
        def _(i):
            h, n = lax.div(i, tiles), lax.rem(i, tiles)
            some = pl.ds(pl.multiple_of(y * c_n * rows, c_n * rows), c_n * rows)
            columns = pl.ds(pl.multiple_of(n * wide_n, wide_n), wide_n)
            turned[h, some, columns] = jnp.dot(
                gathered[h, some, :], rot[h, :, columns], preferred_element_type=F32
            ).astype(BF16)

    sibling = jnp.bitwise_xor(ti, 1)
    for h in range(zh_n):
        got_g(sibling, h).wait_recv()
    turn(yi)

    quarters = s4s.shape[1]
    each = z_n // quarters

    def quarter(q, k):
        per = quarters // zh_n
        return chosen.at[
            lax.div(q, per),
            pl.ds(pl.multiple_of(k * held, held), held),
            pl.ds(pl.multiple_of(lax.rem(q, per) * each * piece, each * piece), each * piece),
        ]

    def send4(x, q):
        return remote(quarter(q, xi), quarter(q, xi), s4s.at[x, q], s4r.at[xi, q], at(x=x))

    home = lax.div(zi, each)
    for j in (0, 1, quarters - 1, 2):
        q = lax.rem(home + j, quarters)

        @pl.loop(0, each)
        def _(i):
            z = q * each + i

            @pl.when(z != zi)
            def _():
                remote(chunk(z, xi), chunk(z, xi), s3s.at[z], s3r.at[z], at()).wait_recv()

        @pl.loop(1, x_n)
        def _(i):
            send4(lax.rem(xi + i, x_n), q).start()

    for j in range(1, y_n):
        y = lax.rem(yi + (j if j < 2 else y_n + 1 - j), y_n)
        for c in range(c_n):
            for h in range(zh_n):
                got_g(y * c_n + c, h).wait_recv()
        turn(y)

    @pl.loop(1, x_n)
    def _(i):
        x = lax.rem(xi + i, x_n)
        for q in range(quarters):
            remote(quarter(q, x), quarter(q, x), s4s.at[x, q], s4r.at[x, q], at()).wait_recv()

    @pl.loop(0, zh_n * tiles)
    def _(i):
        h, n = lax.div(i, tiles), lax.rem(i, tiles)
        columns = pl.ds(pl.multiple_of(n * wide_n, wide_n), wide_n)
        damping = 0.1 * jnp.mean(eigs[h], axis=1, keepdims=True)
        product = jnp.dot(chosen[h], rot[h, :, columns], preferred_element_type=F32)
        asked[h, :, columns] = (product / (eigs[h, :, columns] + damping)).astype(BF16)

    def score(y):
        some = pl.ds(pl.multiple_of(y * c_n * rows, c_n * rows), c_n * rows)
        total = None
        for h in range(zh_n):
            term = lax.dot_general(
                turned[h, some, :], asked[h], (((1,), (1,)), ((), ())), preferred_element_type=F32
            )
            total = term if total is None else total + term
        part[pl.ds(y * c_n, c_n)] = total.reshape(c_n, rows, total.shape[1])

    def send_p(t):
        return remote(part.at[t], parts.at[ti], sps.at[t], spr.at[ti], at(t=t))

    @pl.loop(1, y_n)
    def _(j):
        y = lax.rem(yi + j, y_n)
        score(y)
        for c in range(c_n):
            send_p(y * c_n + c).start()

    score(yi)
    send_p(sibling).start()
    parts[ti] = part[ti]

    @pl.loop(1, t_n)
    def _(i):
        t = jnp.bitwise_xor(ti, i)
        remote(parts.at[t], parts.at[t], sps.at[t], spr.at[t], at()).wait_recv()

    total = parts[0]
    for t in range(1, t_n):
        total += parts[t]
    out_ref[...] = total * (1.0 / math.sqrt(modules * width))

    @pl.loop(1, zl_n)
    def _(i):
        send1(lax.rem(zl + i, zl_n)).wait_send()

    @pl.loop(1, z_n)
    def _(i):
        send3(lax.rem(zi + i, z_n)).wait_send()

    @pl.loop(1, x_n)
    def _(i):
        x = lax.rem(xi + i, x_n)
        send2(x).wait_send()
        for q in range(quarters):
            send4(x, q).wait_send()

    @pl.loop(1, t_n)
    def _(i):
        t = jnp.bitwise_xor(ti, i)
        send_p(t).wait_send()
        for h in range(zh_n):
            send_g(t, h).wait_send()


def local(dims, train_grads, query_grads, basis_out, basis_in, eigenvalues, owner_groups, module_order):
    zl_n, x_n, zh_n, y_n, c_n = dims
    rows, modules, width = train_grads.shape
    held, side = query_grads.shape[1], basis_out.shape[1]
    t_n, z_n, piece = y_n * c_n, zh_n * zl_n, width // zl_n
    asks = owner_groups.shape[0] * held
    vmem, smem = pl.BlockSpec(memory_space=pltpu.VMEM), pl.BlockSpec(memory_space=pltpu.SMEM)
    dma = pltpu.SemaphoreType.DMA
    return pl.pallas_call(
        functools.partial(kernel, dims),
        out_shape=jax.ShapeDtypeStruct((rows, asks), F32),
        in_specs=[vmem] * 5 + [smem] * 2,
        out_specs=vmem,
        scratch_shapes=[
            pltpu.VMEM((16 * modules, 16 * modules), BF16),
            pltpu.VMEM((modules, rows, width), BF16),
            pltpu.VMEM((zh_n, t_n * rows, width), BF16),
            pltpu.VMEM((zh_n, width, width), BF16),
            pltpu.VMEM((zh_n, t_n * rows, width), BF16),
            pltpu.VMEM((zh_n, 2, side, 128), BF16),
            pltpu.VMEM((zh_n, 1, width), F32),
            pltpu.VMEM((zl_n, held, piece), BF16),
            pltpu.VMEM((x_n, held, piece), BF16),
            pltpu.VMEM((x_n, held, piece), BF16),
            pltpu.VMEM((zh_n, asks, width), BF16),
            pltpu.VMEM((zh_n, asks, width), BF16),
            pltpu.VMEM((t_n, rows, asks), F32),
            pltpu.VMEM((t_n, rows, asks), F32),
            dma((zl_n,)),
            dma((zl_n,)),
            dma((x_n,)),
            dma((x_n,)),
            dma((z_n,)),
            dma((z_n,)),
            dma((x_n, 4)),
            dma((x_n, 4)),
            dma((t_n, zh_n)),
            dma((t_n, zh_n)),
            dma((2,)),
            dma((2,)),
            dma((t_n,)),
            dma((t_n,)),
        ],
        compiler_params=pltpu.CompilerParams(
            collective_id=0, has_side_effects=True, vmem_limit_bytes=40 << 20
        ),
    )(
        train_grads,
        query_grads.reshape(held, width),
        basis_out[0],
        basis_in[0],
        eigenvalues,
        owner_groups,
        module_order,
    )


def solution(mesh, layout=(X, ZH, Y, C)):
    x_n, zh_n, y_n, c_n = layout
    dims = (mesh.shape["group"] // x_n, x_n, zh_n, y_n, c_n)
    in_specs = (
        P(("group", "module"), None, None),
        P("group", None, "module", None),
        P("module", None, None),
        P("module", None, None),
        P("module", None),
        P(),
        P(),
    )
    out_specs = P(("group", "module"), None)
    return jax.shard_map(
        functools.partial(local, dims), mesh=mesh, in_specs=in_specs, out_specs=out_specs, check_vma=False
    )
```

time: 1310 us -> 59.9 us (0.05)
  waiting for transfers between devices: 1230 us -> 0 us
  Pallas kernels: 0 us -> 53.2 us
  local copies, waits for them, and re-layouts: 34.7 us -> 6.44 us
  between operations: 14.8 us -> 0.02 us
    all_gather x1 -> x0, waiting for transfers between devices: 814 us -> none  [local(): everywhere = lax.all_gather(back, ('group', 'module'), axis=0, tiled=True)]
    unnamed x3 -> x0, waiting for transfers between devices: 415 us -> none
    pallas_call x0 -> x1, Pallas kernels: none -> 53.2 us  [local(): pl.pallas_call(functools.partial(kernel, dims), out_shape=jax.ShapeDtypeS...]
  transfers between devices with their start and end apart: 2 -> 0, of which waited for: 2 -> 0; matrix products, arithmetic and copies ran while one was open for 2% -> 0% of each run, Pallas kernels for 0% -> 0%
where the time goes in v2:
time: 59.9 us; the launch traced here: 59.6 us
  Pallas kernels  53.2 us (89%)
  local copies, waits for them, and re-layouts  6.44 us (11%)
    pallas_call x1, Pallas kernels, local(): pl.pallas_call(functools.partial(kernel, dims), out_shape=jax.ShapeDtypeS...  53.2 us
    unnamed x15, local copies, waits for them, and re-layouts  6.44 us

profile of v2, /device:TPU:1, one launch (start us, length us, event | category | flops | bytes accessed | tf_op | source)
XLA Modules:
  0.0 59.6 jit_solution(15381182914630128837)
XLA Ops:
  0.0 0.0 copy-start
  0.0 1.6 %copy-done = bf16[64,16,1024]{2,1,0:T(8,128)(2,1)S(1)} copy-done((bf16[64,16,1024]{2,1,0:T(8,128)(2,1)S(1)}, bf16[64,16,1024]{2,1,0:T(8,128)(2,1)}, u32[]{:S(2)}) %copy-start) | copy-done | bytes 2097176
  1.6 0.0 copy-start.1
  1.6 0.8 %copy-done.1 = bf16[1,32,1,1024]{3,1,2,0:T(8,128)(2,1)S(1)} copy-done((bf16[1,32,1,1024]{3,1,2,0:T(8,128)(2,1)S(1)}, bf16[1,32,1,1024]{3,1,2,0:T(8,128)(2,1)}, u32[]{:S(2)}) %copy-start.1) | copy-done | bytes 65560
  2.4 0.0 copy-start.2
  2.4 0.7 %copy-done.2 = bf16[1,32,32]{2,1,0:T(8,128)(2,1)S(1)} copy-done((bf16[1,32,32]{2,1,0:T(8,128)(2,1)S(1)}, bf16[1,32,32]{2,1,0:T(8,128)(2,1)}, u32[]{:S(2)}) %copy-start.2) | copy-done | bytes 2072
  3.1 0.0 copy-start.3
  3.1 0.7 %copy-done.3 = bf16[1,32,32]{2,1,0:T(8,128)(2,1)S(1)} copy-done((bf16[1,32,32]{2,1,0:T(8,128)(2,1)S(1)}, bf16[1,32,32]{2,1,0:T(8,128)(2,1)}, u32[]{:S(2)}) %copy-start.3) | copy-done | bytes 2072
  3.8 0.0 copy-start.4
  3.8 0.7 %copy-done.4 = f32[1,1024]{1,0:T(1,128)S(1)} copy-done((f32[1,1024]{1,0:T(1,128)S(1)}, f32[1,1024]{1,0:T(1,128)}, u32[]{:S(2)}) %copy-start.4) | copy-done | bytes 4120
  4.5 0.0 copy-start.5
  4.5 0.7 %copy-done.5 = s32[4]{0:T(128)S(1)} copy-done((s32[4]{0:T(128)S(1)}, s32[4]{0:T(128)}, u32[]{:S(2)}) %copy-start.5) | copy-done | bytes 40
  5.2 0.0 copy-start.6
  5.2 0.7 %copy-done.6 = s32[16]{0:T(128)S(1)} copy-done((s32[16]{0:T(128)S(1)}, s32[16]{0:T(128)}, u32[]{:S(2)}) %copy-start.6) | copy-done | bytes 88
  5.8 53.2 %shard_map.73 = f32[64,128]{1,0:T(8,128)S(1)} custom-call(bf16[64,16,1024]{2,1,0:T(8,128)(2,1)S(1)} %copy-done, bf16[32,1024]{1,0:T(8,128)(2,1)S(1)} %bitcast.3, bf16[32,32]{1,0:T(8,128)(2,1)S(1)} %bitcast.4, bf16[32,32]{1,0:T(8,128)(2,1)S(1)} %bitcast.5, f32[1,1024]{1,0:T(1,128)S(1)} %copy-done.4, s32[4]{0:T(128)S(1)} %copy-done.5, s32[16]{0:T(128)S(1)} %copy-done.6), custom_call_target="tpu_custom_call" | custom-call | tf_op jit(solution)/shard_map/pallas_call | solution.py:364
  59.0 0.6 %copy.9 = f32[64,128]{1,0:T(8,128)} copy(f32[64,128]{1,0:T(8,128)S(1)} %shard_map.73) | data formatting | bytes 65536
Async XLA Ops:
  0.0 1.6 %copy-start = (bf16[64,16,1024]{2,1,0:T(8,128)(2,1)S(1)}, bf16[64,16,1024]{2,1,0:T(8,128)(2,1)}, u32[]{:S(2)}) copy-start(bf16[64,16,1024]{2,1,0:T(8,128)(2,1)} %train_ref.1) | copy-start | bytes 6291460
  1.6 0.8 %copy-start.1 = (bf16[1,32,1,1024]{3,1,2,0:T(8,128)(2,1)S(1)}, bf16[1,32,1,1024]{3,1,2,0:T(8,128)(2,1)}, u32[]{:S(2)}) copy-start(bf16[1,32,1,1024]{3,1,2,0:T(8,128)(2,1)} %param.8) | copy-start | bytes 196612
  2.4 0.7 %copy-start.2 = (bf16[1,32,32]{2,1,0:T(8,128)(2,1)S(1)}, bf16[1,32,32]{2,1,0:T(8,128)(2,1)}, u32[]{:S(2)}) copy-start(bf16[1,32,32]{2,1,0:T(8,128)(2,1)} %param.9) | copy-start | bytes 6148
  3.1 0.7 %copy-start.3 = (bf16[1,32,32]{2,1,0:T(8,128)(2,1)S(1)}, bf16[1,32,32]{2,1,0:T(8,128)(2,1)}, u32[]{:S(2)}) copy-start(bf16[1,32,32]{2,1,0:T(8,128)(2,1)} %param.10) | copy-start | bytes 6148
  3.8 0.7 %copy-start.4 = (f32[1,1024]{1,0:T(1,128)S(1)}, f32[1,1024]{1,0:T(1,128)}, u32[]{:S(2)}) copy-start(f32[1,1024]{1,0:T(1,128)} %eig_ref.1) | copy-start | bytes 12292
  4.5 0.7 %copy-start.5 = (s32[4]{0:T(128)S(1)}, s32[4]{0:T(128)}, u32[]{:S(2)}) copy-start(s32[4]{0:T(128)} %owner_ref.1) | copy-start | bytes 52
  5.2 0.7 %copy-start.6 = (s32[16]{0:T(128)S(1)}, s32[16]{0:T(128)}, u32[]{:S(2)}) copy-start(s32[16]{0:T(128)} %order_ref.1) | copy-start | bytes 196

commit v3 on v2

--- a/solution.py
+++ b/solution.py
@@ -15,14 +15,21 @@
 
 def kernel(
     dims,
+    train_hbm,
+    query_hbm,
+    bout_hbm,
+    bin_hbm,
+    eig_hbm,
+    owner_hbm,
+    order_hbm,
+    out_ref,
     train_ref,
     query_ref,
     bout_ref,
     bin_ref,
-    eig_ref,
     owner_ref,
     order_ref,
-    out_ref,
+    fetch_sem,
     perm,
     ordered,
     gathered,
@@ -80,6 +87,23 @@
             device_id_type=pl.DeviceIdType.MESH,
         )
 
+    fetches = [
+        pltpu.make_async_copy(src, dst, fetch_sem.at[i])
+        for i, (src, dst) in enumerate(
+            (
+                (order_hbm, order_ref),
+                (train_hbm, train_ref),
+                (query_hbm, query_ref),
+                (bout_hbm, bout_ref),
+                (bin_hbm, bin_ref),
+                (eig_hbm, eigs.at[zh]),
+                (owner_hbm, owner_ref),
+            )
+        )
+    ]
+    for fetch in fetches:
+        fetch.start()
+
     barrier = pltpu.get_barrier_semaphore()
 
     def greet(where):
@@ -99,6 +123,8 @@
     def _(i):
         greet(at(t=lax.rem(ti + i, t_n)))
 
+    for fetch in fetches:
+        fetch.wait()
     batch = 16
     span = batch * modules
     for s in range(modules):
@@ -114,7 +140,6 @@
     bases[zh] = jnp.zeros(bases.shape[1:], BF16)
     bases[zh, 0, :, : bout_ref.shape[1]] = bout_ref[...]
     bases[zh, 1, :, : bin_ref.shape[1]] = bin_ref[...]
-    eigs[zh] = eig_ref[...]
 
     pl.semaphore_wait(barrier, z_n + x_n + t_n - 3)
 
@@ -157,10 +182,12 @@
             at(t=t),
         )
 
-    @pl.loop(1, t_n)
-    def _(i):
-        for h in range(zh_n):
-            send_g(jnp.bitwise_xor(ti, i), h).start()
+    near = [j for j in range(1, y_n) if j != 2]
+    far = [j for j in range(1, y_n) if j == 2]
+    for j in [0] + near + far:
+        for c in range(1 if j == 0 else 0, c_n):
+            for h in range(zh_n):
+                send_g(jnp.bitwise_xor(ti, j * c_n + c), h).start()
 
     for h in range(zh_n):
         gathered[h, pl.ds(pl.multiple_of(ti * rows, rows), rows)] = ordered[h * t_n + ti]
@@ -275,12 +302,14 @@
         def _(i):
             send4(lax.rem(xi + i, x_n), q).start()
 
-    for j in range(1, y_n):
-        y = lax.rem(yi + (j if j < 2 else y_n + 1 - j), y_n)
+    def await_g(y):
         for c in range(c_n):
             for h in range(zh_n):
                 got_g(y * c_n + c, h).wait_recv()
-        turn(y)
+
+    for j in near:
+        await_g(jnp.bitwise_xor(yi, j))
+        turn(jnp.bitwise_xor(yi, j))
 
     @pl.loop(1, x_n)
     def _(i):
@@ -309,16 +338,18 @@
     def send_p(t):
         return remote(part.at[t], parts.at[ti], sps.at[t], spr.at[ti], at(t=t))
 
-    @pl.loop(1, y_n)
-    def _(j):
-        y = lax.rem(yi + j, y_n)
+    for j in near + [0] + far:
+        y = jnp.bitwise_xor(yi, j)
+        if j in far:
+            await_g(y)
+            turn(y)
         score(y)
         for c in range(c_n):
-            send_p(y * c_n + c).start()
-
-    score(yi)
-    send_p(sibling).start()
-    parts[ti] = part[ti]
+            if j:
+                send_p(y * c_n + c).start()
+        if j == 0:
+            send_p(sibling).start()
+            parts[ti] = part[ti]
 
     @pl.loop(1, t_n)
     def _(i):
@@ -359,14 +390,20 @@
     held, side = query_grads.shape[1], basis_out.shape[1]
     t_n, z_n, piece = y_n * c_n, zh_n * zl_n, width // zl_n
     asks = owner_groups.shape[0] * held
-    vmem, smem = pl.BlockSpec(memory_space=pltpu.VMEM), pl.BlockSpec(memory_space=pltpu.SMEM)
     dma = pltpu.SemaphoreType.DMA
     return pl.pallas_call(
         functools.partial(kernel, dims),
         out_shape=jax.ShapeDtypeStruct((rows, asks), F32),
-        in_specs=[vmem] * 5 + [smem] * 2,
-        out_specs=vmem,
+        in_specs=[pl.BlockSpec(memory_space=pl.ANY)] * 7,
+        out_specs=pl.BlockSpec(memory_space=pltpu.VMEM),
         scratch_shapes=[
+            pltpu.VMEM((rows, modules, width), BF16),
+            pltpu.VMEM((held, width), BF16),
+            pltpu.VMEM((side, side), BF16),
+            pltpu.VMEM((side, side), BF16),
+            pltpu.SMEM(owner_groups.shape, jnp.int32),
+            pltpu.SMEM(module_order.shape, jnp.int32),
+            dma((7,)),
             pltpu.VMEM((16 * modules, 16 * modules), BF16),
             pltpu.VMEM((modules, rows, width), BF16),
             pltpu.VMEM((zh_n, t_n * rows, width), BF16),
@@ -397,7 +434,7 @@
             dma((t_n,)),
         ],
         compiler_params=pltpu.CompilerParams(
-            collective_id=0, has_side_effects=True, vmem_limit_bytes=40 << 20
+            collective_id=0, has_side_effects=True, vmem_limit_bytes=60 << 20
         ),
     )(
         train_grads,

time: 59.9 us -> 55.3 us (0.923)
  local copies, waits for them, and re-layouts: 6.44 us -> 1.38 us
    unnamed x15 -> x1, local copies, waits for them, and re-layouts: 6.44 us -> 1.38 us
where the time goes in v3:
time: 55.3 us; the launch traced here: 55.1 us
  Pallas kernels  53.7 us (97%)
  local copies, waits for them, and re-layouts  1.38 us (2%)
    pallas_call x1, Pallas kernels, local(): pl.pallas_call(functools.partial(kernel, dims), out_shape=jax.ShapeDtypeS...  53.7 us
    unnamed x1, local copies, waits for them, and re-layouts  1.38 us

profile of v3, /device:TPU:1, one launch (start us, length us, event | category | flops | bytes accessed | tf_op | source)
XLA Modules:
  0.0 55.1 jit_solution(7672839800178255370)
XLA Ops:
  0.0 53.7 %shard_map.73 = f32[64,128]{1,0:T(8,128)} custom-call(bf16[64,16,1024]{2,1,0:T(8,128)(2,1)} %train_hbm.1, bf16[32,1024]{1,0:T(8,128)(2,1)} %bitcast.3, bf16[32,32]{1,0:T(8,128)(2,1)} %bitcast.4, bf16[32,32]{1,0:T(8,128)(2,1)} %bitcast.5, f32[1,1024]{1,0:T(1,128)} %eig_hbm.1, s32[4]{0:T(128)} %owner_hbm.1, s32[16]{0:T(128)} %order_hbm.1), custom_call_target="tpu_custom_call" | custom-call | tf_op jit(solution)/shard_map/pallas_call | solution.py:394
  53.7 1.4 %copy.9 = f32[64,128]{1,0:T(8,128)} copy(f32[64,128]{1,0:T(8,128)} %shard_map.73) | data formatting | bytes 65536

commit v4 on v3

--- a/solution.py
+++ b/solution.py
@@ -37,13 +37,15 @@
     turned,
     bases,
     eigs,
-    raw,
+    heard,
+    crossed,
     offer,
     offered,
     chosen,
     asked,
     part,
     parts,
+    whole,
     s1s,
     s1r,
     s2s,
@@ -111,9 +113,8 @@
             barrier, inc=1, device_id=where, device_id_type=pl.DeviceIdType.MESH
         )
 
-    @pl.loop(1, z_n)
-    def _(i):
-        greet(at(z=lax.rem(zi + i, z_n)))
+    greet(at(z=lax.rem(zi + 1, z_n)))
+    greet(at(z=lax.rem(zi + z_n - 1, z_n)))
 
     @pl.loop(1, x_n)
     def _(i):
@@ -123,46 +124,46 @@
     def _(i):
         greet(at(t=lax.rem(ti + i, t_n)))
 
-    for fetch in fetches:
-        fetch.wait()
+    order_in, train_in, query_in, *small_in = fetches
+    query_in.wait()
+    pl.semaphore_wait(barrier, x_n + t_n)
+
+    def send1(x):
+        return remote(query_ref, crossed.at[xi], s1s.at[x], s1r.at[xi], at(x=x))
+
+    @pl.loop(1, x_n)
+    def _(i):
+        send1(lax.rem(xi + i, x_n)).start()
+
+    def tell(step):
+        d = 1 << step
+        for z in (lax.rem(zi + d, z_n), lax.rem(zi + z_n - d, z_n)):
+            pl.semaphore_signal(
+                heard.at[step], inc=1, device_id=at(z=z), device_id_type=pl.DeviceIdType.MESH
+            )
+
+    def hear(step):
+        pl.semaphore_wait(heard.at[step], 2)
+        if step + 1 < steps:
+            tell(step + 1)
+
+    steps = (z_n // 2).bit_length() - 1
+    tell(0)
+
     batch = 16
     span = batch * modules
+    order_in.wait()
     for s in range(modules):
         lane = lax.broadcasted_iota(jnp.int32, (batch, span), 1)
         row = lax.broadcasted_iota(jnp.int32, (batch, span), 0)
         hit = lane == row * modules + order_ref[s]
         perm[pl.ds(s * batch, batch), :] = jnp.where(hit, 1.0, 0.0).astype(BF16)
+    train_in.wait()
     for b in range(rows // batch):
         block = train_ref[pl.ds(b * batch, batch)].reshape(span, width)
         moved = jnp.dot(perm[...], block, preferred_element_type=F32).astype(BF16)
         ordered[:, pl.ds(b * batch, batch), :] = moved.reshape(modules, batch, width)
-
-    bases[zh] = jnp.zeros(bases.shape[1:], BF16)
-    bases[zh, 0, :, : bout_ref.shape[1]] = bout_ref[...]
-    bases[zh, 1, :, : bin_ref.shape[1]] = bin_ref[...]
-
-    pl.semaphore_wait(barrier, z_n + x_n + t_n - 3)
-
-    def send1(z):
-        return remote(
-            query_ref.at[:, pl.ds(pl.multiple_of(z * piece, piece), piece)],
-            raw.at[zl],
-            s1s.at[z],
-            s1r.at[zl],
-            at(z=zh * zl_n + z),
-        )
-
-    @pl.loop(1, zl_n)
-    def _(i):
-        send1(lax.rem(zl + i, zl_n)).start()
-
-    other = zh_n - 1 - zh
-    twins = [
-        remote(bases.at[zh], bases.at[zh], sbs.at[0], sbr.at[0], at(z=other * zl_n + zl)),
-        remote(eigs.at[zh], eigs.at[zh], sbs.at[1], sbr.at[1], at(z=other * zl_n + zl)),
-    ]
-    for twin in twins:
-        twin.start()
+    hear(0)
 
     def send_g(t, h):
         return remote(
@@ -189,8 +190,15 @@
             for h in range(zh_n):
                 send_g(jnp.bitwise_xor(ti, j * c_n + c), h).start()
 
-    for h in range(zh_n):
-        gathered[h, pl.ds(pl.multiple_of(ti * rows, rows), rows)] = ordered[h * t_n + ti]
+    for fetch in small_in:
+        fetch.wait()
+
+    bases[zh] = jnp.zeros(bases.shape[1:], BF16)
+    bases[zh, 0, :, : bout_ref.shape[1]] = bout_ref[...]
+    bases[zh, 1, :, : bin_ref.shape[1]] = bin_ref[...]
+
+    if steps > 1:
+        hear(1)
 
     def build(h):
         side = bout_ref.shape[1]
@@ -205,34 +213,49 @@
 
     build(zh)
 
-    raw[zl] = query_ref[:, pl.ds(pl.multiple_of(zl * piece, piece), piece)]
+    for h in range(zh_n):
+        gathered[h, pl.ds(pl.multiple_of(ti * rows, rows), rows)] = ordered[h * t_n + ti]
+
+    crossed[xi] = query_ref[...]
+
+    @pl.loop(1, x_n)
+    def _(i):
+        x = lax.rem(xi + i, x_n)
+        remote(query_ref, crossed.at[x], s1s.at[x], s1r.at[x], at()).wait_recv()
+
+    offer[...] = crossed[lax.rem(owner_ref[xi], x_n)]
+    for step in range(min(2, steps), steps):
+        hear(step)
+
+    def span_of(z):
+        return pl.ds(pl.multiple_of(z * piece, piece), piece)
+
+    def send2(z):
+        return remote(
+            offer.at[:, span_of(z)], offered.at[zl], s2s.at[z], s2r.at[zl], at(z=zh * zl_n + z)
+        )
 
     @pl.loop(1, zl_n)
     def _(i):
+        send2(lax.rem(zl + i, zl_n)).start()
+
+    other = zh_n - 1 - zh
+    twins = [
+        remote(bases.at[zh], bases.at[zh], sbs.at[0], sbr.at[0], at(z=other * zl_n + zl)),
+        remote(eigs.at[zh], eigs.at[zh], sbs.at[1], sbr.at[1], at(z=other * zl_n + zl)),
+    ]
+    for twin in twins:
+        twin.start()
+
+    offered[zl] = offer[:, span_of(zl)]
+
+    @pl.loop(1, zl_n)
+    def _(i):
         z = lax.rem(zl + i, zl_n)
-        remote(raw.at[z], raw.at[z], s1s.at[z], s1r.at[z], at()).wait_recv()
-
-    for k in range(x_n):
-        offer[k] = raw[lax.div(owner_ref[k], x_n)]
-
-    def send2(x):
-        return remote(offer.at[x], offered.at[xi], s2s.at[x], s2r.at[xi], at(x=x))
-
-    @pl.loop(1, x_n)
-    def _(i):
-        send2(lax.rem(xi + i, x_n)).start()
-
-    offered[xi] = offer[xi]
-
-    @pl.loop(1, x_n)
-    def _(i):
-        x = lax.rem(xi + i, x_n)
-        remote(offer.at[x], offered.at[x], s2s.at[x], s2r.at[x], at()).wait_recv()
+        remote(offered.at[z], offered.at[z], s2s.at[z], s2r.at[z], at()).wait_recv()
 
     lines = pl.ds(pl.multiple_of(xi * held, held), held)
-    chosen[zh, lines, pl.ds(pl.multiple_of(zl * piece, piece), piece)] = offered[
-        lax.rem(owner_ref[xi], x_n)
-    ]
+    chosen[zh, lines, span_of(zl)] = offered[lax.div(owner_ref[xi], x_n)]
 
     def chunk(z, k):
         return chosen.at[
@@ -333,7 +356,8 @@
                 turned[h, some, :], asked[h], (((1,), (1,)), ((), ())), preferred_element_type=F32
             )
             total = term if total is None else total + term
-        part[pl.ds(y * c_n, c_n)] = total.reshape(c_n, rows, total.shape[1])
+        part[pl.ds(y * c_n, c_n)] = total.reshape(c_n, rows, total.shape[1]).astype(BF16)
+        return total
 
     def send_p(t):
         return remote(part.at[t], parts.at[ti], sps.at[t], spr.at[ti], at(t=t))
@@ -343,27 +367,27 @@
         if j in far:
             await_g(y)
             turn(y)
-        score(y)
+        total = score(y)
         for c in range(c_n):
             if j:
                 send_p(y * c_n + c).start()
         if j == 0:
             send_p(sibling).start()
-            parts[ti] = part[ti]
+            whole[...] = total.reshape(c_n, rows, total.shape[1])
 
     @pl.loop(1, t_n)
     def _(i):
         t = jnp.bitwise_xor(ti, i)
         remote(parts.at[t], parts.at[t], sps.at[t], spr.at[t], at()).wait_recv()
 
-    total = parts[0]
-    for t in range(1, t_n):
-        total += parts[t]
+    total = whole[lax.rem(ti, c_n)]
+    for i in range(1, t_n):
+        total += parts[jnp.bitwise_xor(ti, i)].astype(F32)
     out_ref[...] = total * (1.0 / math.sqrt(modules * width))
 
     @pl.loop(1, zl_n)
     def _(i):
-        send1(lax.rem(zl + i, zl_n)).wait_send()
+        send2(lax.rem(zl + i, zl_n)).wait_send()
 
     @pl.loop(1, z_n)
     def _(i):
@@ -372,7 +396,7 @@
     @pl.loop(1, x_n)
     def _(i):
         x = lax.rem(xi + i, x_n)
-        send2(x).wait_send()
+        send1(x).wait_send()
         for q in range(quarters):
             send4(x, q).wait_send()
 
@@ -411,17 +435,19 @@
             pltpu.VMEM((zh_n, t_n * rows, width), BF16),
             pltpu.VMEM((zh_n, 2, side, 128), BF16),
             pltpu.VMEM((zh_n, 1, width), F32),
+            pltpu.SemaphoreType.REGULAR(((z_n // 2).bit_length() - 1,)),
+            pltpu.VMEM((x_n, held, width), BF16),
+            pltpu.VMEM((held, width), BF16),
             pltpu.VMEM((zl_n, held, piece), BF16),
-            pltpu.VMEM((x_n, held, piece), BF16),
-            pltpu.VMEM((x_n, held, piece), BF16),
             pltpu.VMEM((zh_n, asks, width), BF16),
             pltpu.VMEM((zh_n, asks, width), BF16),
-            pltpu.VMEM((t_n, rows, asks), F32),
-            pltpu.VMEM((t_n, rows, asks), F32),
+            pltpu.VMEM((t_n, rows, asks), BF16),
+            pltpu.VMEM((t_n, rows, asks), BF16),
+            pltpu.VMEM((c_n, rows, asks), F32),
+            dma((x_n,)),
+            dma((x_n,)),
             dma((zl_n,)),
             dma((zl_n,)),
-            dma((x_n,)),
-            dma((x_n,)),
             dma((z_n,)),
             dma((z_n,)),
             dma((x_n, 4)),

time: 55.3 us -> 53.6 us (0.969)
  Pallas kernels: 53.7 us -> 52 us
    pallas_call x1, Pallas kernels: 53.7 us -> 52 us  [local(): pl.pallas_call(functools.partial(kernel, dims), out_shape=jax.ShapeDtypeS...]
where the time goes in v4:
time: 53.6 us; the launch traced here: 53.4 us
  Pallas kernels  52 us (97%)
  local copies, waits for them, and re-layouts  1.38 us (3%)
    pallas_call x1, Pallas kernels, local(): pl.pallas_call(functools.partial(kernel, dims), out_shape=jax.ShapeDtypeS...  52 us
    unnamed x1, local copies, waits for them, and re-layouts  1.38 us

profile of v4, /device:TPU:1, one launch (start us, length us, event | category | flops | bytes accessed | tf_op | source)
XLA Modules:
  0.0 53.4 jit_solution(6135401206011860118)
XLA Ops:
  0.0 52.0 %shard_map.73 = f32[64,128]{1,0:T(8,128)} custom-call(bf16[64,16,1024]{2,1,0:T(8,128)(2,1)} %train_hbm.1, bf16[32,1024]{1,0:T(8,128)(2,1)} %bitcast.3, bf16[32,32]{1,0:T(8,128)(2,1)} %bitcast.4, bf16[32,32]{1,0:T(8,128)(2,1)} %bitcast.5, f32[1,1024]{1,0:T(1,128)} %eig_hbm.1, s32[4]{0:T(128)} %owner_hbm.1, s32[16]{0:T(128)} %order_hbm.1), custom_call_target="tpu_custom_call" | custom-call | tf_op jit(solution)/shard_map/pallas_call | solution.py:418
  52.0 1.4 %copy.9 = f32[64,128]{1,0:T(8,128)} copy(f32[64,128]{1,0:T(8,128)} %shard_map.73) | data formatting | bytes 65536

commit v5 on v4

--- a/solution.py
+++ b/solution.py
@@ -43,6 +43,7 @@
     offered,
     chosen,
     asked,
+    total_asked,
     part,
     parts,
     whole,
@@ -194,20 +195,20 @@
         fetch.wait()
 
     bases[zh] = jnp.zeros(bases.shape[1:], BF16)
-    bases[zh, 0, :, : bout_ref.shape[1]] = bout_ref[...]
-    bases[zh, 1, :, : bin_ref.shape[1]] = bin_ref[...]
+    side = bout_ref.shape[1]
+    bases[zh, :, :side] = bout_ref[...]
+    bases[zh, :, side : 2 * side] = bin_ref[...]
 
     if steps > 1:
         hear(1)
 
     def build(h):
-        side = bout_ref.shape[1]
-        lane = lax.broadcasted_iota(jnp.int32, (bases.shape[3], width), 1)
-        row = lax.broadcasted_iota(jnp.int32, (bases.shape[3], width), 0)
+        lane = lax.broadcasted_iota(jnp.int32, (bases.shape[2], width), 1)
+        row = lax.broadcasted_iota(jnp.int32, (bases.shape[2], width), 0)
         wide = jnp.where(lax.div(lane, side) == row, 1.0, 0.0).astype(BF16)
-        tiled = jnp.where(lax.rem(lane, side) == row, 1.0, 0.0).astype(BF16)
-        outer = jnp.dot(bases[h, 0], wide, preferred_element_type=F32)
-        inner = jnp.dot(bases[h, 1], tiled, preferred_element_type=F32)
+        tiled = jnp.where(lax.rem(lane, side) + side == row, 1.0, 0.0).astype(BF16)
+        outer = jnp.dot(bases[h], wide, preferred_element_type=F32)
+        inner = jnp.dot(bases[h], tiled, preferred_element_type=F32)
         for a in range(side):
             rot[h, pl.ds(a * side, side), :] = (outer[a : a + 1] * inner).astype(BF16)
 
@@ -241,8 +242,8 @@
 
     other = zh_n - 1 - zh
     twins = [
-        remote(bases.at[zh], bases.at[zh], sbs.at[0], sbr.at[0], at(z=other * zl_n + zl)),
-        remote(eigs.at[zh], eigs.at[zh], sbs.at[1], sbr.at[1], at(z=other * zl_n + zl)),
+        remote(bases.at[zh], bases.at[zh], sbs.at[0], sbr.at[0], at(z=z_n - 1 - zi)),
+        remote(eigs.at[zh], eigs.at[zh], sbs.at[1], sbr.at[1], at(z=z_n - 1 - zi)),
     ]
     for twin in twins:
         twin.start()
@@ -277,23 +278,19 @@
         remote(buf.at[other], buf.at[other], sbs.at[i], sbr.at[i], at()).wait_recv()
     build(other)
 
-    wide_n = 256
-    tiles = width // wide_n
-
     def turn(y):
-        @pl.loop(0, zh_n * tiles)
-        def _(i):
-            h, n = lax.div(i, tiles), lax.rem(i, tiles)
+        @pl.loop(0, zh_n)
+        def _(h):
             some = pl.ds(pl.multiple_of(y * c_n * rows, c_n * rows), c_n * rows)
-            columns = pl.ds(pl.multiple_of(n * wide_n, wide_n), wide_n)
-            turned[h, some, columns] = jnp.dot(
-                gathered[h, some, :], rot[h, :, columns], preferred_element_type=F32
+            turned[h, some, :] = jnp.dot(
+                gathered[h, some, :], rot[h], preferred_element_type=F32
             ).astype(BF16)
 
     sibling = jnp.bitwise_xor(ti, 1)
     for h in range(zh_n):
         got_g(sibling, h).wait_recv()
     turn(yi)
+    total_asked[...] = jnp.zeros_like(total_asked)
 
     quarters = s4s.shape[1]
     each = z_n // quarters
@@ -310,8 +307,8 @@
         return remote(quarter(q, xi), quarter(q, xi), s4s.at[x, q], s4r.at[xi, q], at(x=x))
 
     home = lax.div(zi, each)
-    for j in (0, 1, quarters - 1, 2):
-        q = lax.rem(home + j, quarters)
+    order = [lax.rem(home + j, quarters) for j in (0, 1, quarters - 1, 2)]
+    for q in order:
 
         @pl.loop(0, each)
         def _(i):
@@ -334,19 +331,23 @@
         await_g(jnp.bitwise_xor(yi, j))
         turn(jnp.bitwise_xor(yi, j))
 
-    @pl.loop(1, x_n)
-    def _(i):
-        x = lax.rem(xi + i, x_n)
-        for q in range(quarters):
+    half = each * piece
+    for q in order:
+
+        @pl.loop(1, x_n)
+        def _(i):
+            x = lax.rem(xi + i, x_n)
             remote(quarter(q, x), quarter(q, x), s4s.at[x, q], s4r.at[x, q], at()).wait_recv()
 
-    @pl.loop(0, zh_n * tiles)
-    def _(i):
-        h, n = lax.div(i, tiles), lax.rem(i, tiles)
-        columns = pl.ds(pl.multiple_of(n * wide_n, wide_n), wide_n)
+        h = lax.div(q, quarters // zh_n)
+        these = pl.ds(pl.multiple_of(lax.rem(q, quarters // zh_n) * half, half), half)
+        total_asked[h] += jnp.dot(
+            chosen[h, :, these], rot[h, these, :], preferred_element_type=F32
+        )
+
+    for h in range(zh_n):
         damping = 0.1 * jnp.mean(eigs[h], axis=1, keepdims=True)
-        product = jnp.dot(chosen[h], rot[h, :, columns], preferred_element_type=F32)
-        asked[h, :, columns] = (product / (eigs[h, :, columns] + damping)).astype(BF16)
+        asked[h] = (total_asked[h] / (eigs[h] + damping)).astype(BF16)
 
     def score(y):
         some = pl.ds(pl.multiple_of(y * c_n * rows, c_n * rows), c_n * rows)
@@ -362,7 +363,7 @@
     def send_p(t):
         return remote(part.at[t], parts.at[ti], sps.at[t], spr.at[ti], at(t=t))
 
-    for j in near + [0] + far:
+    for j in near + far + [0]:
         y = jnp.bitwise_xor(yi, j)
         if j in far:
             await_g(y)
@@ -375,6 +376,26 @@
             send_p(sibling).start()
             whole[...] = total.reshape(c_n, rows, total.shape[1])
 
+    @pl.loop(1, zl_n)
+    def _(i):
+        send2(lax.rem(zl + i, zl_n)).wait_send()
+
+    @pl.loop(1, z_n)
+    def _(i):
+        send3(lax.rem(zi + i, z_n)).wait_send()
+
+    @pl.loop(1, x_n)
+    def _(i):
+        x = lax.rem(xi + i, x_n)
+        send1(x).wait_send()
+        for q in range(quarters):
+            send4(x, q).wait_send()
+
+    @pl.loop(1, t_n)
+    def _(i):
+        for h in range(zh_n):
+            send_g(jnp.bitwise_xor(ti, i), h).wait_send()
+
     @pl.loop(1, t_n)
     def _(i):
         t = jnp.bitwise_xor(ti, i)
@@ -385,27 +406,9 @@
         total += parts[jnp.bitwise_xor(ti, i)].astype(F32)
     out_ref[...] = total * (1.0 / math.sqrt(modules * width))
 
-    @pl.loop(1, zl_n)
-    def _(i):
-        send2(lax.rem(zl + i, zl_n)).wait_send()
-
-    @pl.loop(1, z_n)
-    def _(i):
-        send3(lax.rem(zi + i, z_n)).wait_send()
-
-    @pl.loop(1, x_n)
-    def _(i):
-        x = lax.rem(xi + i, x_n)
-        send1(x).wait_send()
-        for q in range(quarters):
-            send4(x, q).wait_send()
-
     @pl.loop(1, t_n)
     def _(i):
-        t = jnp.bitwise_xor(ti, i)
-        send_p(t).wait_send()
-        for h in range(zh_n):
-            send_g(t, h).wait_send()
+        send_p(jnp.bitwise_xor(ti, i)).wait_send()
 
 
 def local(dims, train_grads, query_grads, basis_out, basis_in, eigenvalues, owner_groups, module_order):
@@ -433,7 +436,7 @@
             pltpu.VMEM((zh_n, t_n * rows, width), BF16),
             pltpu.VMEM((zh_n, width, width), BF16),
             pltpu.VMEM((zh_n, t_n * rows, width), BF16),
-            pltpu.VMEM((zh_n, 2, side, 128), BF16),
+            pltpu.VMEM((zh_n, side, 128), BF16),
             pltpu.VMEM((zh_n, 1, width), F32),
             pltpu.SemaphoreType.REGULAR(((z_n // 2).bit_length() - 1,)),
             pltpu.VMEM((x_n, held, width), BF16),
@@ -441,6 +444,7 @@
             pltpu.VMEM((zl_n, held, piece), BF16),
             pltpu.VMEM((zh_n, asks, width), BF16),
             pltpu.VMEM((zh_n, asks, width), BF16),
+            pltpu.VMEM((zh_n, asks, width), F32),
             pltpu.VMEM((t_n, rows, asks), BF16),
             pltpu.VMEM((t_n, rows, asks), BF16),
             pltpu.VMEM((c_n, rows, asks), F32),

time: 53.6 us -> 49.7 us (0.927)
  Pallas kernels: 52 us -> 48.2 us
    pallas_call x1, Pallas kernels: 52 us -> 48.2 us  [local(): pl.pallas_call(functools.partial(kernel, dims), out_shape=jax.ShapeDtypeS...]
where the time goes in v5:
time: 49.7 us; the launch traced here: 49.5 us
  Pallas kernels  48.2 us (97%)
  local copies, waits for them, and re-layouts  1.38 us (3%)
    pallas_call x1, Pallas kernels, local(): pl.pallas_call(functools.partial(kernel, dims), out_shape=jax.ShapeDtypeS...  48.2 us
    unnamed x1, local copies, waits for them, and re-layouts  1.38 us

profile of v5, /device:TPU:1, one launch (start us, length us, event | category | flops | bytes accessed | tf_op | source)
XLA Modules:
  0.0 49.5 jit_solution(7345469202752610724)
XLA Ops:
  0.0 48.2 %shard_map.73 = f32[64,128]{1,0:T(8,128)} custom-call(bf16[64,16,1024]{2,1,0:T(8,128)(2,1)} %train_hbm.1, bf16[32,1024]{1,0:T(8,128)(2,1)} %bitcast.3, bf16[32,32]{1,0:T(8,128)(2,1)} %bitcast.4, bf16[32,32]{1,0:T(8,128)(2,1)} %bitcast.5, f32[1,1024]{1,0:T(1,128)} %eig_hbm.1, s32[4]{0:T(128)} %owner_hbm.1, s32[16]{0:T(128)} %order_hbm.1), custom_call_target="tpu_custom_call" | custom-call | tf_op jit(solution)/shard_map/pallas_call | solution.py:421
  48.2 1.4 %copy.9 = f32[64,128]{1,0:T(8,128)} copy(f32[64,128]{1,0:T(8,128)} %shard_map.73) | data formatting | bytes 65536

commit v6 on v5

--- a/solution.py
+++ b/solution.py
@@ -43,7 +43,7 @@
     offered,
     chosen,
     asked,
-    total_asked,
+    divisor,
     part,
     parts,
     whole,
@@ -67,7 +67,10 @@
     z_n = zh_n * zl_n
     rows, modules, width = train_ref.shape
     held = query_ref.shape[0]
-    piece = width // zl_n
+    owners = owner_hbm.shape[0]
+    per = zl_n // owners
+    wide_x = width // x_n
+    piece = wide_x // per
     group, module = lax.axis_index("group"), lax.axis_index("module")
     zl, xi = lax.div(group, x_n), lax.rem(group, x_n)
     zh, ti = lax.div(module, t_n), lax.rem(module, t_n)
@@ -114,8 +117,9 @@
             barrier, inc=1, device_id=where, device_id_type=pl.DeviceIdType.MESH
         )
 
-    greet(at(z=lax.rem(zi + 1, z_n)))
-    greet(at(z=lax.rem(zi + z_n - 1, z_n)))
+    around = sorted({1, 2, z_n - 2, z_n - 1})
+    for i in around:
+        greet(at(z=lax.rem(zi + i, z_n)))
 
     @pl.loop(1, x_n)
     def _(i):
@@ -127,17 +131,22 @@
 
     order_in, train_in, query_in, *small_in = fetches
     query_in.wait()
-    pl.semaphore_wait(barrier, x_n + t_n)
+    pl.semaphore_wait(barrier, len(around) + x_n + t_n - 2)
+
+    def columns_of(x):
+        return pl.ds(pl.multiple_of(x * wide_x, wide_x), wide_x)
 
     def send1(x):
-        return remote(query_ref, crossed.at[xi], s1s.at[x], s1r.at[xi], at(x=x))
+        return remote(
+            query_ref.at[:, columns_of(x)], crossed.at[xi], s1s.at[x], s1r.at[xi], at(x=x)
+        )
 
     @pl.loop(1, x_n)
     def _(i):
         send1(lax.rem(xi + i, x_n)).start()
 
     def tell(step):
-        d = 1 << step
+        d = 2 << step
         for z in (lax.rem(zi + d, z_n), lax.rem(zi + z_n - d, z_n)):
             pl.semaphore_signal(
                 heard.at[step], inc=1, device_id=at(z=z), device_id_type=pl.DeviceIdType.MESH
@@ -148,8 +157,9 @@
         if step + 1 < steps:
             tell(step + 1)
 
-    steps = (z_n // 2).bit_length() - 1
-    tell(0)
+    steps = (z_n // 2).bit_length() - 2
+    if steps:
+        tell(0)
 
     batch = 16
     span = batch * modules
@@ -164,7 +174,8 @@
         block = train_ref[pl.ds(b * batch, batch)].reshape(span, width)
         moved = jnp.dot(perm[...], block, preferred_element_type=F32).astype(BF16)
         ordered[:, pl.ds(b * batch, batch), :] = moved.reshape(modules, batch, width)
-    hear(0)
+    if steps:
+        hear(0)
 
     def send_g(t, h):
         return remote(
@@ -187,8 +198,8 @@
     near = [j for j in range(1, y_n) if j != 2]
     far = [j for j in range(1, y_n) if j == 2]
     for j in [0] + near + far:
-        for c in range(1 if j == 0 else 0, c_n):
-            for h in range(zh_n):
+        for h in range(zh_n):
+            for c in range(1 if j == 0 else 0, c_n):
                 send_g(jnp.bitwise_xor(ti, j * c_n + c), h).start()
 
     for fetch in small_in:
@@ -198,9 +209,6 @@
     side = bout_ref.shape[1]
     bases[zh, :, :side] = bout_ref[...]
     bases[zh, :, side : 2 * side] = bin_ref[...]
-
-    if steps > 1:
-        hear(1)
 
     def build(h):
         lane = lax.broadcasted_iota(jnp.int32, (bases.shape[2], width), 1)
@@ -217,23 +225,29 @@
     for h in range(zh_n):
         gathered[h, pl.ds(pl.multiple_of(ti * rows, rows), rows)] = ordered[h * t_n + ti]
 
-    crossed[xi] = query_ref[...]
+    crossed[xi] = query_ref[:, columns_of(xi)]
 
     @pl.loop(1, x_n)
     def _(i):
         x = lax.rem(xi + i, x_n)
-        remote(query_ref, crossed.at[x], s1s.at[x], s1r.at[x], at()).wait_recv()
-
-    offer[...] = crossed[lax.rem(owner_ref[xi], x_n)]
-    for step in range(min(2, steps), steps):
+        remote(crossed.at[x], crossed.at[x], s1s.at[x], s1r.at[x], at()).wait_recv()
+
+    for k in range(owners):
+        offer[k] = crossed[lax.rem(owner_ref[k], x_n)]
+    for step in range(1, steps):
         hear(step)
 
-    def span_of(z):
-        return pl.ds(pl.multiple_of(z * piece, piece), piece)
+    def lines_of(k, n=1):
+        return pl.ds(pl.multiple_of(k * held, n * held), n * held)
 
     def send2(z):
+        part_z = pl.ds(pl.multiple_of(lax.rem(z, per) * piece, piece), piece)
         return remote(
-            offer.at[:, span_of(z)], offered.at[zl], s2s.at[z], s2r.at[zl], at(z=zh * zl_n + z)
+            offer.at[lax.div(z, per), :, part_z],
+            offered.at[zl],
+            s2s.at[z],
+            s2r.at[zl],
+            at(z=zh * zl_n + z),
         )
 
     @pl.loop(1, zl_n)
@@ -248,22 +262,27 @@
     for twin in twins:
         twin.start()
 
-    offered[zl] = offer[:, span_of(zl)]
+    mine = lax.div(zl, per)
+    offered[zl] = offer[mine, :, pl.ds(pl.multiple_of(lax.rem(zl, per) * piece, piece), piece)]
 
     @pl.loop(1, zl_n)
     def _(i):
         z = lax.rem(zl + i, zl_n)
         remote(offered.at[z], offered.at[z], s2s.at[z], s2r.at[z], at()).wait_recv()
 
-    lines = pl.ds(pl.multiple_of(xi * held, held), held)
-    chosen[zh, lines, span_of(zl)] = offered[lax.div(owner_ref[xi], x_n)]
-
-    def chunk(z, k):
-        return chosen.at[
+    def place(z, x):
+        zz = lax.rem(z, zl_n)
+        start = x * wide_x + lax.rem(zz, per) * piece
+        return (
             lax.div(z, zl_n),
-            pl.ds(pl.multiple_of(k * held, held), held),
-            pl.ds(pl.multiple_of(lax.rem(z, zl_n) * piece, piece), piece),
-        ]
+            lines_of(lax.div(zz, per)),
+            pl.ds(pl.multiple_of(start, piece), piece),
+        )
+
+    def chunk(z, x):
+        return chosen.at[place(z, x)]
+
+    chosen[place(zi, xi)] = offered[lax.div(owner_ref[mine], x_n)]
 
     def send3(z):
         return remote(chunk(zi, xi), chunk(zi, xi), s3s.at[z], s3r.at[zi], at(z=z))
@@ -278,76 +297,67 @@
         remote(buf.at[other], buf.at[other], sbs.at[i], sbr.at[i], at()).wait_recv()
     build(other)
 
-    def turn(y):
-        @pl.loop(0, zh_n)
-        def _(h):
-            some = pl.ds(pl.multiple_of(y * c_n * rows, c_n * rows), c_n * rows)
-            turned[h, some, :] = jnp.dot(
-                gathered[h, some, :], rot[h], preferred_element_type=F32
-            ).astype(BF16)
+    def turn_slot(y, h):
+        some = pl.ds(pl.multiple_of(y * c_n * rows, c_n * rows), c_n * rows)
+        turned[h, some, :] = jnp.dot(
+            gathered[h, some, :], rot[h], preferred_element_type=F32
+        ).astype(BF16)
 
     sibling = jnp.bitwise_xor(ti, 1)
     for h in range(zh_n):
         got_g(sibling, h).wait_recv()
-    turn(yi)
-    total_asked[...] = jnp.zeros_like(total_asked)
-
-    quarters = s4s.shape[1]
-    each = z_n // quarters
-
-    def quarter(q, k):
-        per = quarters // zh_n
-        return chosen.at[
-            lax.div(q, per),
-            pl.ds(pl.multiple_of(k * held, held), held),
-            pl.ds(pl.multiple_of(lax.rem(q, per) * each * piece, each * piece), each * piece),
-        ]
-
-    def send4(x, q):
-        return remote(quarter(q, xi), quarter(q, xi), s4s.at[x, q], s4r.at[xi, q], at(x=x))
-
-    home = lax.div(zi, each)
-    order = [lax.rem(home + j, quarters) for j in (0, 1, quarters - 1, 2)]
+
+    @pl.loop(0, zh_n)
+    def _(h):
+        turn_slot(yi, h)
+
+    for h in range(zh_n):
+        divisor[h] = eigs[h] + 0.1 * jnp.mean(eigs[h], axis=1, keepdims=True)
+
+    def block(e, x):
+        return chosen.at[lax.div(e, owners), lines_of(lax.rem(e, owners)), columns_of(x)]
+
+    def send4(x, e):
+        return remote(block(e, xi), block(e, xi), s4s.at[x, e], s4r.at[xi, e], at(x=x))
+
+    blocks = s4s.shape[1]
+    quarters = blocks // 2
+    home = lax.div(zi, 2 * per)
+    nearest = (0, 1, 3, 2) if quarters == 4 else range(quarters)
+    order = [lax.rem(home + j, quarters) for j in nearest]
     for q in order:
 
-        @pl.loop(0, each)
-        def _(i):
-            z = q * each + i
-
-            @pl.when(z != zi)
-            def _():
-                remote(chunk(z, xi), chunk(z, xi), s3s.at[z], s3r.at[z], at()).wait_recv()
-
-        @pl.loop(1, x_n)
-        def _(i):
-            send4(lax.rem(xi + i, x_n), q).start()
-
-    def await_g(y):
-        for c in range(c_n):
-            for h in range(zh_n):
+        @pl.loop(2 * q, 2 * q + 2)
+        def _(e):
+            for i in range(per):
+                z = e * per + i
+
+                @pl.when(z != zi)
+                def _():
+                    remote(chunk(z, xi), chunk(z, xi), s3s.at[z], s3r.at[z], at()).wait_recv()
+
+            for i in range(1, x_n):
+                send4(lax.rem(xi + i, x_n), e).start()
+
+    def turn_got(y):
+        @pl.loop(0, zh_n)
+        def _(h):
+            for c in range(c_n):
                 got_g(y * c_n + c, h).wait_recv()
+            turn_slot(y, h)
 
     for j in near:
-        await_g(jnp.bitwise_xor(yi, j))
-        turn(jnp.bitwise_xor(yi, j))
-
-    half = each * piece
+        turn_got(jnp.bitwise_xor(yi, j))
+
     for q in order:
-
-        @pl.loop(1, x_n)
-        def _(i):
-            x = lax.rem(xi + i, x_n)
-            remote(quarter(q, x), quarter(q, x), s4s.at[x, q], s4r.at[x, q], at()).wait_recv()
-
-        h = lax.div(q, quarters // zh_n)
-        these = pl.ds(pl.multiple_of(lax.rem(q, quarters // zh_n) * half, half), half)
-        total_asked[h] += jnp.dot(
-            chosen[h, :, these], rot[h, these, :], preferred_element_type=F32
-        )
-
-    for h in range(zh_n):
-        damping = 0.1 * jnp.mean(eigs[h], axis=1, keepdims=True)
-        asked[h] = (total_asked[h] / (eigs[h] + damping)).astype(BF16)
+        for e in (2 * q, 2 * q + 1):
+            for i in range(1, x_n):
+                x = lax.rem(xi + i, x_n)
+                remote(block(e, x), block(e, x), s4s.at[x, e], s4r.at[x, e], at()).wait_recv()
+        h = lax.div(2 * q, owners)
+        these = lines_of(lax.rem(2 * q, owners), 2)
+        product = jnp.dot(chosen[h, these, :], rot[h], preferred_element_type=F32)
+        asked[h, these, :] = (product / divisor[h]).astype(BF16)
 
     def score(y):
         some = pl.ds(pl.multiple_of(y * c_n * rows, c_n * rows), c_n * rows)
@@ -366,8 +376,7 @@
     for j in near + far + [0]:
         y = jnp.bitwise_xor(yi, j)
         if j in far:
-            await_g(y)
-            turn(y)
+            turn_got(y)
         total = score(y)
         for c in range(c_n):
             if j:
@@ -388,8 +397,8 @@
     def _(i):
         x = lax.rem(xi + i, x_n)
         send1(x).wait_send()
-        for q in range(quarters):
-            send4(x, q).wait_send()
+        for e in range(blocks):
+            send4(x, e).wait_send()
 
     @pl.loop(1, t_n)
     def _(i):
@@ -415,8 +424,8 @@
     zl_n, x_n, zh_n, y_n, c_n = dims
     rows, modules, width = train_grads.shape
     held, side = query_grads.shape[1], basis_out.shape[1]
-    t_n, z_n, piece = y_n * c_n, zh_n * zl_n, width // zl_n
-    asks = owner_groups.shape[0] * held
+    t_n, z_n, owners = y_n * c_n, zh_n * zl_n, owner_groups.shape[0]
+    asks, wide_x, piece = owners * held, width // x_n, width // x_n // (zl_n // owners)
     dma = pltpu.SemaphoreType.DMA
     return pl.pallas_call(
         functools.partial(kernel, dims),
@@ -438,13 +447,13 @@
             pltpu.VMEM((zh_n, t_n * rows, width), BF16),
             pltpu.VMEM((zh_n, side, 128), BF16),
             pltpu.VMEM((zh_n, 1, width), F32),
-            pltpu.SemaphoreType.REGULAR(((z_n // 2).bit_length() - 1,)),
-            pltpu.VMEM((x_n, held, width), BF16),
-            pltpu.VMEM((held, width), BF16),
+            pltpu.SemaphoreType.REGULAR((max(1, (z_n // 2).bit_length() - 2),)),
+            pltpu.VMEM((x_n, held, wide_x), BF16),
+            pltpu.VMEM((owners, held, wide_x), BF16),
             pltpu.VMEM((zl_n, held, piece), BF16),
             pltpu.VMEM((zh_n, asks, width), BF16),
             pltpu.VMEM((zh_n, asks, width), BF16),
-            pltpu.VMEM((zh_n, asks, width), F32),
+            pltpu.VMEM((zh_n, 1, width), F32),
             pltpu.VMEM((t_n, rows, asks), BF16),
             pltpu.VMEM((t_n, rows, asks), BF16),
             pltpu.VMEM((c_n, rows, asks), F32),
@@ -454,8 +463,8 @@
             dma((zl_n,)),
             dma((z_n,)),
             dma((z_n,)),
-            dma((x_n, 4)),
-            dma((x_n, 4)),
+            dma((x_n, zh_n * owners)),
+            dma((x_n, zh_n * owners)),
             dma((t_n, zh_n)),
             dma((t_n, zh_n)),
             dma((2,)),

time: 49.7 us -> 50.1 us (level)
  no operation moved by 1% of the time
where the time goes in v6:
time: 50.1 us; the launch traced here: 49.9 us
  Pallas kernels  48.5 us (97%)
  local copies, waits for them, and re-layouts  1.38 us (3%)
    pallas_call x1, Pallas kernels, local(): pl.pallas_call(functools.partial(kernel, dims), out_shape=jax.ShapeDtypeS...  48.5 us
    unnamed x1, local copies, waits for them, and re-layouts  1.38 us

profile of v6, /device:TPU:1, one launch (start us, length us, event | category | flops | bytes accessed | tf_op | source)
XLA Modules:
  0.0 49.9 jit_solution(15743849512945583783)
XLA Ops:
  0.0 48.5 %shard_map.73 = f32[64,128]{1,0:T(8,128)} custom-call(bf16[64,16,1024]{2,1,0:T(8,128)(2,1)} %train_hbm.1, bf16[32,1024]{1,0:T(8,128)(2,1)} %bitcast.3, bf16[32,32]{1,0:T(8,128)(2,1)} %bitcast.4, bf16[32,32]{1,0:T(8,128)(2,1)} %bitcast.5, f32[1,1024]{1,0:T(1,128)} %eig_hbm.1, s32[4]{0:T(128)} %owner_hbm.1, s32[16]{0:T(128)} %order_hbm.1), custom_call_target="tpu_custom_call" | custom-call | tf_op jit(solution)/shard_map/pallas_call | solution.py:430
  48.5 1.4 %copy.9 = f32[64,128]{1,0:T(8,128)} copy(f32[64,128]{1,0:T(8,128)} %shard_map.73) | data formatting | bytes 65536

commit v7 on v6

--- a/solution.py
+++ b/solution.py
@@ -130,36 +130,6 @@
         greet(at(t=lax.rem(ti + i, t_n)))
 
     order_in, train_in, query_in, *small_in = fetches
-    query_in.wait()
-    pl.semaphore_wait(barrier, len(around) + x_n + t_n - 2)
-
-    def columns_of(x):
-        return pl.ds(pl.multiple_of(x * wide_x, wide_x), wide_x)
-
-    def send1(x):
-        return remote(
-            query_ref.at[:, columns_of(x)], crossed.at[xi], s1s.at[x], s1r.at[xi], at(x=x)
-        )
-
-    @pl.loop(1, x_n)
-    def _(i):
-        send1(lax.rem(xi + i, x_n)).start()
-
-    def tell(step):
-        d = 2 << step
-        for z in (lax.rem(zi + d, z_n), lax.rem(zi + z_n - d, z_n)):
-            pl.semaphore_signal(
-                heard.at[step], inc=1, device_id=at(z=z), device_id_type=pl.DeviceIdType.MESH
-            )
-
-    def hear(step):
-        pl.semaphore_wait(heard.at[step], 2)
-        if step + 1 < steps:
-            tell(step + 1)
-
-    steps = (z_n // 2).bit_length() - 2
-    if steps:
-        tell(0)
 
     batch = 16
     span = batch * modules
@@ -174,8 +144,36 @@
         block = train_ref[pl.ds(b * batch, batch)].reshape(span, width)
         moved = jnp.dot(perm[...], block, preferred_element_type=F32).astype(BF16)
         ordered[:, pl.ds(b * batch, batch), :] = moved.reshape(modules, batch, width)
+    query_in.wait()
+    pl.semaphore_wait(barrier, len(around) + x_n + t_n - 2)
+
+    def columns_of(x):
+        return pl.ds(pl.multiple_of(x * wide_x, wide_x), wide_x)
+
+    def send1(x):
+        return remote(
+            query_ref.at[:, columns_of(x)], crossed.at[xi], s1s.at[x], s1r.at[xi], at(x=x)
+        )
+
+    @pl.loop(1, x_n)
+    def _(i):
+        send1(lax.rem(xi + i, x_n)).start()
+
+    def tell(step):
+        d = 2 << step
+        for z in (lax.rem(zi + d, z_n), lax.rem(zi + z_n - d, z_n)):
+            pl.semaphore_signal(
+                heard.at[step], inc=1, device_id=at(z=z), device_id_type=pl.DeviceIdType.MESH
+            )
+
+    def hear(step):
+        pl.semaphore_wait(heard.at[step], 2)
+        if step + 1 < steps:
+            tell(step + 1)
+
+    steps = (z_n // 2).bit_length() - 2
     if steps:
-        hear(0)
+        tell(0)
 
     def send_g(t, h):
         return remote(
@@ -202,6 +200,8 @@
             for c in range(1 if j == 0 else 0, c_n):
                 send_g(jnp.bitwise_xor(ti, j * c_n + c), h).start()
 
+    if steps:
+        hear(0)
     for fetch in small_in:
         fetch.wait()
 
@@ -287,9 +287,12 @@
     def send3(z):
         return remote(chunk(zi, xi), chunk(zi, xi), s3s.at[z], s3r.at[zi], at(z=z))
 
-    @pl.loop(1, z_n)
-    def _(i):
-        send3(lax.rem(zi + i, z_n)).start()
+    send3(lax.rem(zi + z_n // 2, z_n)).start()
+
+    @pl.loop(1, z_n // 2)
+    def _(i):
+        send3(lax.rem(zi + z_n // 2 - i, z_n)).start()
+        send3(lax.rem(zi + z_n // 2 + i, z_n)).start()
 
     for twin in twins:
         twin.wait_send()

time: 50.1 us -> 49.2 us (0.982)
  Pallas kernels: 48.5 us -> 47.7 us
    pallas_call x1, Pallas kernels: 48.5 us -> 47.7 us  [local(): pl.pallas_call(functools.partial(kernel, dims), out_shape=jax.ShapeDtypeS...]
where the time goes in v7:
time: 49.2 us; the launch traced here: 49 us
  Pallas kernels  47.7 us (97%)
  local copies, waits for them, and re-layouts  1.38 us (3%)
    pallas_call x1, Pallas kernels, local(): pl.pallas_call(functools.partial(kernel, dims), out_shape=jax.ShapeDtypeS...  47.7 us
    unnamed x1, local copies, waits for them, and re-layouts  1.38 us

profile of v7, /device:TPU:1, one launch (start us, length us, event | category | flops | bytes accessed | tf_op | source)
XLA Modules:
  0.0 49.0 jit_solution(12002561371266346797)
XLA Ops:
  0.0 47.7 %shard_map.73 = f32[64,128]{1,0:T(8,128)} custom-call(bf16[64,16,1024]{2,1,0:T(8,128)(2,1)} %train_hbm.1, bf16[32,1024]{1,0:T(8,128)(2,1)} %bitcast.3, bf16[32,32]{1,0:T(8,128)(2,1)} %bitcast.4, bf16[32,32]{1,0:T(8,128)(2,1)} %bitcast.5, f32[1,1024]{1,0:T(1,128)} %eig_hbm.1, s32[4]{0:T(128)} %owner_hbm.1, s32[16]{0:T(128)} %order_hbm.1), custom_call_target="tpu_custom_call" | custom-call | tf_op jit(solution)/shard_map/pallas_call | solution.py:433
  47.7 1.4 %copy.9 = f32[64,128]{1,0:T(8,128)} copy(f32[64,128]{1,0:T(8,128)} %shard_map.73) | data formatting | bytes 65536

commit v8 on v7

--- a/solution.py
+++ b/solution.py
@@ -308,13 +308,6 @@
 
     sibling = jnp.bitwise_xor(ti, 1)
     for h in range(zh_n):
-        got_g(sibling, h).wait_recv()
-
-    @pl.loop(0, zh_n)
-    def _(h):
-        turn_slot(yi, h)
-
-    for h in range(zh_n):
         divisor[h] = eigs[h] + 0.1 * jnp.mean(eigs[h], axis=1, keepdims=True)
 
     def block(e, x):
@@ -326,7 +319,7 @@
     blocks = s4s.shape[1]
     quarters = blocks // 2
     home = lax.div(zi, 2 * per)
-    nearest = (0, 1, 3, 2) if quarters == 4 else range(quarters)
+    nearest = (2, 1, 3, 0) if quarters == 4 else range(quarters)
     order = [lax.rem(home + j, quarters) for j in nearest]
     for q in order:
 
@@ -341,6 +334,13 @@
 
             for i in range(1, x_n):
                 send4(lax.rem(xi + i, x_n), e).start()
+
+    for h in range(zh_n):
+        got_g(sibling, h).wait_recv()
+
+    @pl.loop(0, zh_n)
+    def _(h):
+        turn_slot(yi, h)
 
     def turn_got(y):
         @pl.loop(0, zh_n)

time: 49.2 us -> 49.3 us (level)
  no operation moved by 1% of the time
where the time goes in v8:
time: 49.3 us; the launch traced here: 49.1 us
  Pallas kernels  47.7 us (97%)
  local copies, waits for them, and re-layouts  1.38 us (3%)
    pallas_call x1, Pallas kernels, local(): pl.pallas_call(functools.partial(kernel, dims), out_shape=jax.ShapeDtypeS...  47.7 us
    unnamed x1, local copies, waits for them, and re-layouts  1.38 us

profile of v8, /device:TPU:1, one launch (start us, length us, event | category | flops | bytes accessed | tf_op | source)
XLA Modules:
  0.0 49.1 jit_solution(11124422632466137264)
XLA Ops:
  0.0 47.7 %shard_map.73 = f32[64,128]{1,0:T(8,128)} custom-call(bf16[64,16,1024]{2,1,0:T(8,128)(2,1)} %train_hbm.1, bf16[32,1024]{1,0:T(8,128)(2,1)} %bitcast.3, bf16[32,32]{1,0:T(8,128)(2,1)} %bitcast.4, bf16[32,32]{1,0:T(8,128)(2,1)} %bitcast.5, f32[1,1024]{1,0:T(1,128)} %eig_hbm.1, s32[4]{0:T(128)} %owner_hbm.1, s32[16]{0:T(128)} %order_hbm.1), custom_call_target="tpu_custom_call" | custom-call | tf_op jit(solution)/shard_map/pallas_call | solution.py:433
  47.7 1.4 %copy.9 = f32[64,128]{1,0:T(8,128)} copy(f32[64,128]{1,0:T(8,128)} %shard_map.73) | data formatting | bytes 65536
